TPU v7x, 32 devices: a whole 2x2x4 slice. The times are simulated.
32 devices in a mesh: stream: 2 (over y), seq: 8 (over z, core), tensor: 2 (over x).
Axes of the slice: x: 2, y: 2, z: 4, core: 2. Of those that a mesh axis runs over, the one named last changes fastest.
Arguments:
- hidden: bfloat16 [2, 1, 4096, 4096], P('stream', None, 'seq', 'tensor'), may hold values from -32 to 32
- norm_gain: float32 [4096], replicated, may hold values from 0.1 to 1.9
- query_weight: bfloat16 [4096, 4096], P('seq', 'tensor'), may hold values from -1 to 1
- key_weight: bfloat16 [4096, 1024], P('seq', 'tensor'), may hold values from -24 to 24
- value_projection_weight: bfloat16 [4096, 1024], P('seq', 'tensor'), may hold values from -0.09375 to 0.09375
- out_weight: bfloat16 [4096, 4096], P('tensor', 'seq'), may hold values from -0.125 to 0.125
Outputs:
- cross_out: bfloat16 [2, 1, 4096, 4096], P('stream', None, 'seq', 'tensor')
All inputs are finite; a program needn't handle non-finite values.
Results may differ from a plain program's by a relative error of at most 0.014.
The roundings to bfloat16 on the way count: a program that leaves them out, or rounds other values in their place, can miss the bound.
Values may be sent and summed in bfloat16 or wider, within the bound.
A program may use at most 256 MiB of HBM per device.

v0:
```python
import jax
import jax.numpy as jnp
from jax import lax
from jax.sharding import PartitionSpec as P

HEAD_DIM = 128


def swapped(block, axis, stride):
    count = lax.axis_size(axis)
    route = []
    for low in range(count):
        high = low | 1 << stride
        if high != low and high < count:
            route += [(low, high), (high, low)]
    return lax.ppermute(block, axis, route)


def online_update(running, query_heads, key_block, value_block, query_frame):
    maximum, totals, accumulated = running
    windows, key_count, key_width = key_block.shape
    heads_kv = query_heads.shape[1]
    head_size = query_heads.shape[3]
    key_heads = key_block.reshape(windows, key_count, heads_kv, head_size)
    value_heads = value_block.reshape(windows, key_count, heads_kv, head_size)
    scores = jnp.einsum(
        "bkrd,bnkd->bkrn", query_heads, key_heads, preferred_element_type=jnp.float32
    ) * head_size ** (-0.5)
    key_frame = jnp.arange(key_count, dtype=jnp.int32)
    allowed = key_frame[None, :] <= query_frame[:, None]
    scores = jnp.where(allowed, scores, -1e30)
    fresh = jnp.maximum(maximum, jnp.max(scores, axis=-1))
    expo = jnp.where(allowed, jnp.exp(scores - fresh[..., None]), 0.0)
    totals = jnp.sum(expo, axis=-1)
    product = jnp.einsum(
        "bkrn,bnkd->bkrd",
        expo.astype(jnp.bfloat16),
        value_heads,
        preferred_element_type=jnp.float32,
    )
    accumulated = product
    return (fresh, totals, accumulated)


def body(hidden, norm_gain, query_weight, key_weight, value_projection_weight, out_weight):
    windows = hidden.shape[1]
    frame_count = hidden.shape[2]
    gathered = lax.all_gather(hidden, "tensor", axis=3, tiled=True)
    model_width = gathered.shape[3]
    flat_rows = gathered.reshape(windows * frame_count, model_width).astype(jnp.float32)
    inverse_rms = lax.rsqrt(jnp.mean(flat_rows * flat_rows, axis=1, keepdims=True) + 1e-05)
    normed = (flat_rows * inverse_rms * norm_gain).astype(jnp.bfloat16)
    full_query, full_key, full_value, full_out = (
        lax.all_gather(query_weight, "seq", axis=0, tiled=True),
        lax.all_gather(key_weight, "seq", axis=0, tiled=True),
        lax.all_gather(value_projection_weight, "seq", axis=0, tiled=True),
        lax.all_gather(out_weight, "seq", axis=1, tiled=True),
    )
    query_sum = jnp.dot(normed, full_query, preferred_element_type=jnp.float32)
    key_sum = jnp.dot(normed, full_key, preferred_element_type=jnp.float32)
    value_sum = jnp.dot(normed, full_value, preferred_element_type=jnp.float32)
    query_rows = query_sum.astype(jnp.bfloat16)
    self_key_rows = key_sum.astype(jnp.bfloat16).reshape(windows, frame_count, key_weight.shape[1])
    self_value_rows = value_sum.astype(jnp.bfloat16).reshape(
        windows, frame_count, value_projection_weight.shape[1]
    )
    partner_keys, partner_values = swapped((self_key_rows, self_value_rows), "stream", 0)
    heads_kv = key_weight.shape[1] // HEAD_DIM
    group_repeat = query_weight.shape[1] // (heads_kv * HEAD_DIM)
    query_heads = (
        query_rows.reshape(windows, frame_count, heads_kv, group_repeat, HEAD_DIM)
        .transpose(0, 2, 3, 1, 4)
        .reshape(windows, heads_kv, group_repeat * frame_count, HEAD_DIM)
    )
    query_start = lax.axis_index("seq") * frame_count
    query_frame = query_start + jnp.tile(jnp.arange(frame_count, dtype=jnp.int32), group_repeat)
    initial = (
        jnp.full((windows, heads_kv, group_repeat * frame_count), -1e30, jnp.float32),
        jnp.zeros((windows, heads_kv, group_repeat * frame_count), jnp.float32),
        jnp.zeros((windows, heads_kv, group_repeat * frame_count, HEAD_DIM), jnp.float32),
    )
    query_end = query_start + frame_count
    pieces = (
        lax.all_gather(partner_keys, "seq", axis=1, tiled=True),
        lax.all_gather(partner_values, "seq", axis=1, tiled=True),
    )

    def taken(current):
        return online_update(current, query_heads, pieces[0], pieces[1], query_frame)

    def skipped(current):
        return current

    maximum, totals, accumulated = lax.cond(jnp.int32(0) < query_end, taken, skipped, initial)
    attended_output = (accumulated / totals[..., None]).astype(jnp.bfloat16)
    attended_output = (
        attended_output.reshape(windows, heads_kv, group_repeat, frame_count, HEAD_DIM)
        .transpose(0, 3, 1, 2, 4)
        .reshape(windows * frame_count, heads_kv * group_repeat * HEAD_DIM)
    )
    partial_out = jnp.dot(attended_output, full_out, preferred_element_type=jnp.float32)
    summed = lax.psum_scatter(
        partial_out.astype(jnp.bfloat16), "tensor", scatter_dimension=1, tiled=True
    ).astype(jnp.float32)
    return summed.astype(jnp.bfloat16).reshape(1, windows, frame_count, summed.shape[1])


def solution(mesh):
    in_specs = (
        P("stream", None, "seq", "tensor"),
        P(),
        P("seq", "tensor"),
        P("seq", "tensor"),
        P("seq", "tensor"),
        P("tensor", "seq"),
    )
    out_specs = P("stream", None, "seq", "tensor")
    return jax.shard_map(body, mesh=mesh, in_specs=in_specs, out_specs=out_specs, check_vma=False)
```

profile of v0, /device:TPU:0, one launch (start us, length us, event | category | flops | bytes accessed | tf_op | source)
XLA Modules:
  0.0 665.1 jit_solution(13722145855826253714)
XLA Ops:
  6.5 0.7 all-gather.8.cloned.1.call-update
  7.3 0.7 all-gather.12.cloned.1.call-update
  9.4 59.0 %all-gather.8.cloned.1.call-done = bf16[1,1,512,4096]{3,2,1,0:T(8,128)(2,1)} async-done(((bf16[1,1,512,2048]{3,2,1,0:T(8,128)(2,1)}), bf16[1,1,512,4096]{3,2,1,0:T(8,128)(2,1)}) %all-gather.8.cloned.1.call-update) | async-done | bytes 4194320 | tf_op jit(solution)/shard_map/all_gather | solution.py:48
  68.4 3.1 fusion.17
  71.5 45.7 %all-gather.12.cloned.1.call-done = bf16[4096,512]{1,0:T(8,128)(2,1)} async-done(((bf16[512,512]{1,0:T(8,128)(2,1)}), bf16[4096,512]{1,0:T(8,128)(2,1)}) %all-gather.12.cloned.1.call-update) | async-done | bytes 4194320 | tf_op jit(solution)/shard_map/all_gather | solution.py:55
  117.2 5.8 fusion.20
  123.0 1.5 collective-permute-start
  124.6 12.6 %collective-permute-done = bf16[1,512,512]{2,1,0:T(8,128)(2,1)S(1)} collective-permute-done((bf16[1,512,512]{2,1,0:T(8,128)(2,1)S(1)}, bf16[1,512,512]{2,1,0:T(8,128)(2,1)S(1)}, u32[]{:S(2)}, u32[]{:S(2)}) %collective-permute-start) | collective-permute-done | bytes 524320 | tf_op jit(solution)/shard_map/ppermute | solution.py:16
  137.2 0.8 copy-done.1
  138.0 26.6 %all-gather.16.cloned.1.call-done = bf16[4096,512]{1,0:T(8,128)(2,1)} async-done(((bf16[512,512]{1,0:T(8,128)(2,1)}), bf16[4096,512]{1,0:T(8,128)(2,1)}) %all-gather.16.cloned.1.call-update) | async-done | bytes 4194320 | tf_op jit(solution)/shard_map/all_gather | solution.py:56
  164.7 5.8 fusion.21
  170.5 1.5 collective-permute-start.1
  172.1 12.6 %collective-permute-done.1 = bf16[1,512,512]{2,1,0:T(8,128)(2,1)S(1)} collective-permute-done((bf16[1,512,512]{2,1,0:T(8,128)(2,1)S(1)}, bf16[1,512,512]{2,1,0:T(8,128)(2,1)S(1)}, u32[]{:S(2)}, u32[]{:S(2)}) %collective-permute-start.1) | collective-permute-done | bytes 524320 | tf_op jit(solution)/shard_map/ppermute | solution.py:16
  184.7 0.8 copy-done.2
  185.5 0.7 all-gather.20.cloned.1.call-update
  186.5 129.5 %all-gather.10.cloned.1.call-done = bf16[4096,2048]{1,0:T(8,128)(2,1)} async-done(((bf16[512,2048]{1,0:T(8,128)(2,1)}), bf16[4096,2048]{1,0:T(8,128)(2,1)}) %all-gather.10.cloned.1.call-update) | async-done | bytes 16777232 | tf_op jit(solution)/shard_map/all_gather | solution.py:54
  316.0 14.6 %convolution_convert_fusion.1 = bf16[512,2048]{1,0:T(8,128)(2,1)} fusion(bf16[4096,2048]{1,0:T(8,128)(2,1)} %all-gather.10.cloned.1.call-done, bf16[1,1,512,4096]{3,2,1,0:T(8,128)(2,1)} %all-gather.8.cloned.1.call-done, f32[4096]{0:T(1024)S(1)} %copy-done.3, f32[512]{0:T(512)S(1)} %add_rsqrt_fusion), kind=kOutput, calls=%fused_computation.24 | convolution fusion | flops 8599371776 | bytes 23087104 | tf_op jit(solution)/shard_map/dot_general | solution.py:59
  330.6 3.2 reshape.72
  333.9 1.9 copy.27
  335.7 27.1 %all-gather.14.cloned.1.call-done = bf16[1,4096,512]{2,1,0:T(8,128)(2,1)} async-done(((bf16[1,512,512]{2,1,0:T(8,128)(2,1)}), bf16[1,4096,512]{2,1,0:T(8,128)(2,1)}) %all-gather.14.cloned.1.call-update) | async-done | bytes 4194320 | tf_op jit(solution)/shard_map/all_gather | solution.py:84
  362.8 47.4 %all-gather.18.cloned.1.call-done = bf16[1,4096,512]{2,1,0:T(8,128)(2,1)} async-done(((bf16[1,512,512]{2,1,0:T(8,128)(2,1)}), bf16[1,4096,512]{2,1,0:T(8,128)(2,1)}) %all-gather.18.cloned.1.call-update) | async-done | bytes 4194320 | tf_op jit(solution)/shard_map/all_gather | solution.py:85
  410.2 174.7 %conditional.1 = (f32[1,4,2048]{2,1,0:T(4,128)}, f32[1,4,2048,128]{3,2,1,0:T(8,128)}) conditional(s32[]{:T(128)} %convert_element_type.33, () %tuple.13, (s32[]{:T(128)}, s32[4,512]{1,0:T(4,128)S(1)}, bf16[1,4,4,512,128]{4,3,2,1,0:T(8,128)(2,1)}, bf16[1,4096,512]{2,1,0:T(8,128)(2,1)}, bf16[1,4096,512]{2,1,0:T(8,128)(2,1)}) %tuple.34), branch_computations={%region_1.0_spmd, %region_2.5_spmd} | conditional | flops 17624459264 | bytes 476291136 | solution.py:94
  410.2 11.0 %iota_compare_fusion = pred[2048,4096]{1,0:T(8,128)(4,1)} fusion(s32[2048]{0:T(1024)S(1)} %bitcast.37), kind=kLoop, calls=%fused_computation.7 | loop fusion | flops 8388608 | bytes 8396800 | tf_op jit(solution)/shard_map/cond/branch_1_fun/le | solution.py:30
  421.2 7.1 %reshape.64 = bf16[4096,4,128]{2,1,0:T(4,128)(2,1)} reshape(bf16[1,4096,512]{2,1,0:T(8,128)(2,1)} %get-tuple-element.22) | data formatting | bytes 8388608 | tf_op jit(solution)/shard_map/reshape.1
  428.3 51.1 %fusion = (f32[4,2048]{1,0:T(4,128)S(1)}, f32[4,2048,4096]{2,1,0:T(8,128)}) fusion(pred[2048,4096]{1,0:T(8,128)(4,1)} %iota_compare_fusion, bf16[4,2048,128]{2,1,0:T(8,128)(2,1)S(1)} %bitcast.35, bf16[4096,4,128]{2,1,0:T(4,128)(2,1)} %reshape.64), kind=kOutput, calls=%fused_computation.2 | convolution fusion | flops 8690589696 | bytes 148930560 | tf_op jit(solution)/shard_map/cond/branch_1_fun/bkrd,bnkd->bkrn/dot_general | solution.py:26
  479.4 7.0 %reshape.65 = bf16[4096,4,128]{2,1,0:T(4,128)(2,1)} reshape(bf16[1,4096,512]{2,1,0:T(8,128)(2,1)} %get-tuple-element.23) | data formatting | bytes 8388608 | tf_op jit(solution)/shard_map/reshape.5
  486.3 54.0 %fusion.9 = f32[1,4,2048,128]{3,2,1,0:T(8,128)} fusion(bf16[4096,4,128]{2,1,0:T(4,128)(2,1)} %reshape.65, f32[4,2048,4096]{2,1,0:T(8,128)} %get-tuple-element.29, f32[4,2048]{1,0:T(4,128)S(1)} %broadcast_maximum_fusion, pred[2048,4096]{1,0:T(8,128)(4,1)} %iota_compare_fusion), kind=kOutput, calls=%fused_computation.11 | convolution fusion | flops 8757706752 | bytes 151027712 | tf_op jit(solution)/shard_map/cond/branch_1_fun/bkrn,bnkd->bkrd/dot_general | solution.py:35
  540.3 44.5 %fusion.2 = f32[4,2048]{1,0:T(4,128)} fusion(f32[4,2048,4096]{2,1,0:T(8,128)} %get-tuple-element.29, f32[4,2048]{1,0:T(4,128)S(1)} %broadcast_maximum_fusion, pred[2048,4096]{1,0:T(8,128)(4,1)} %iota_compare_fusion), kind=kLoop, calls=%fused_computation.4 | loop fusion | flops 167763968 | bytes 142671872 | tf_op jit(solution)/shard_map/cond/branch_1_fun/reduce_sum | solution.py:34
  584.9 2.9 divide_convert_fusion
  587.7 2.3 copy.16
  590.1 14.5 %convolution_convert_fusion = bf16[512,4096]{1,0:T(8,128)(2,1)} fusion(bf16[512,2048]{0,1:T(8,128)(2,1)} %bitcast.36, bf16[2048,4096]{1,0:T(8,128)(2,1)} %all-gather.20.cloned.1.call-done), kind=kOutput, calls=%fused_computation.22 | convolution fusion | flops 8592031744 | bytes 23068672 | tf_op jit(solution)/shard_map/dot_general | solution.py:101
  604.6 53.6 %reduce-scatter.2.cloned.1.call-done = bf16[512,2048]{1,0:T(8,128)(2,1)} async-done(((bf16[512,4096]{1,0:T(8,128)(2,1)}), bf16[512,2048]{1,0:T(8,128)(2,1)}) %reduce-scatter.2.cloned.1.call-update) | async-done | bytes 2097168 | tf_op jit(solution)/shard_map/reduce_scatter | solution.py:102
  (25 shorter events, 1.8 us)
Async XLA Ops:
  6.5 110.6 %copy-start.3 = (f32[4096]{0:T(1024)S(1)}, f32[4096]{0:T(1024)}, u32[]{:S(2)}) copy-start(f32[4096]{0:T(1024)} %param.9) | copy-start | bytes 49156
  6.5 61.8 %all-gather.8.cloned.1.call-start = ((), (), s32[]{:S(2)}) async-start(), calls=%async_computation.1 | async-start | bytes 6291456 | tf_op jit(solution)/shard_map/all_gather | solution.py:48
  7.3 109.9 %all-gather.12.cloned.1.call-start = ((), (), s32[]{:S(2)}) async-start(), calls=%async_computation.3 | async-start | bytes 4718592 | tf_op jit(solution)/shard_map/all_gather | solution.py:55
  8.0 156.7 %all-gather.16.cloned.1.call-start = ((), (), s32[]{:S(2)}) async-start(), calls=%async_computation.5 | async-start | bytes 4718592 | tf_op jit(solution)/shard_map/all_gather | solution.py:56
  8.7 307.2 %all-gather.10.cloned.1.call-start = ((), (), s32[]{:S(2)}) async-start(), calls=%async_computation.2 | async-start | bytes 18874368 | tf_op jit(solution)/shard_map/all_gather | solution.py:54
  9.3 353.5 %all-gather.14.cloned.1.call-start = ((), (), s32[]{:S(2)}) async-start(), calls=%async_computation.4 | async-start | bytes 4718592 | tf_op jit(solution)/shard_map/all_gather | solution.py:84
  123.0 14.1 %collective-permute-start = (bf16[1,512,512]{2,1,0:T(8,128)(2,1)S(1)}, bf16[1,512,512]{2,1,0:T(8,128)(2,1)S(1)}, u32[]{:S(2)}, u32[]{:S(2)}) collective-permute-start(bf16[1,512,512]{2,1,0:T(8,128)(2,1)S(1)} %fusion.20), channel_id=1, source_target_pairs={{0,16},{16,0},{1,17},{17,1},{2,18},{18,2},{3,19},{19,3},{4,20},{20... | collective-permute-start | bytes 1572872 | tf_op jit(solution)/shard_map/ppermute | solution.py:16
  137.1 0.8 copy-start.1
  138.0 272.2 %all-gather.18.cloned.1.call-start = ((), (), s32[]{:S(2)}) async-start(), calls=%async_computation.6 | async-start | bytes 4718592 | tf_op jit(solution)/shard_map/all_gather | solution.py:85
  170.5 14.1 %collective-permute-start.1 = (bf16[1,512,512]{2,1,0:T(8,128)(2,1)S(1)}, bf16[1,512,512]{2,1,0:T(8,128)(2,1)S(1)}, u32[]{:S(2)}, u32[]{:S(2)}) collective-permute-start(bf16[1,512,512]{2,1,0:T(8,128)(2,1)S(1)} %fusion.21), channel_id=1, source_target_pairs={{0,16},{16,0},{1,17},{17,1},{2,18},{18,2},{3,19},{19,3},{4,20},{20... | collective-permute-start | bytes 1572872 | tf_op jit(solution)/shard_map/ppermute | solution.py:16
  184.6 0.8 copy-start.2
  185.5 404.6 %all-gather.20.cloned.1.call-start = ((), (), s32[]{:S(2)}) async-start(), calls=%async_computation.7 | async-start | bytes 18874368 | tf_op jit(solution)/shard_map/all_gather | solution.py:57
  186.2 472.0 %reduce-scatter.2.cloned.1.call-start = ((), (), s32[]{:S(2)}) async-start(), calls=%async_computation.8 | async-start | bytes 6291456 | tf_op jit(solution)/shard_map/reduce_scatter | solution.py:102
  410.2 18.0 %copy-start = (bf16[1,4,4,512,128]{4,3,2,1,0:T(8,128)(2,1)S(1)}, bf16[1,4,4,512,128]{4,3,2,1,0:T(8,128)(2,1)}, u32[]{:S(2)}) copy-start(bf16[1,4,4,512,128]{4,3,2,1,0:T(8,128)(2,1)} %get-tuple-element.21) | copy-start | bytes 6291460 | tf_op jit(solution)/shard_map/cond
Sparse Core Ops, SparseCore 0:
  8.9 59.4 all-gather.7
  70.0 47.1 all-gather.11
  118.8 45.8 all-gather.15
  166.1 149.8 all-gather.9
  317.4 45.3 all-gather.13
  364.3 45.8 all-gather.17
  411.8 149.8 all-gather.19
  604.7 53.4 reduce-scatter.1
where the time goes:
time: 666 us; the launch traced here: 665 us
  waiting for transfers between devices  418 us (63%)
  matrix products  146 us (22%)
  other arithmetic  61.5 us (9%)
  local copies, waits for them, and re-layouts  23.1 us (3%)
  between operations  13.5 us (2%)
    all_gather x1, waiting for transfers between devices, body(): lax.all_gather(query_weight, 'seq', axis=0, tiled=True)  130 us
    all_gather x1, waiting for transfers between devices, body(): gathered = lax.all_gather(hidden, 'tensor', axis=3, tiled=True)  59 us
    dot_general x1, matrix products, online_update(): jnp.einsum('bkrn,bnkd->bkrd', expo.astype(jnp.bfloat16), value_heads, pre...  54 us
    reduce_scatter x1, waiting for transfers between devices, body(): lax.psum_scatter(partial_out.astype(jnp.bfloat16), 'tensor', scatter_dime...  53.6 us
    dot_general x1, matrix products, online_update(): jnp.einsum('bkrd,bnkd->bkrn', query_heads, key_heads, preferred_element_t...  51.1 us
    all_gather x1, waiting for transfers between devices, body(): lax.all_gather(partner_values, 'seq', axis=1, tiled=True)  47.4 us
    all_gather x1, waiting for transfers between devices, body(): lax.all_gather(key_weight, 'seq', axis=0, tiled=True)  45.7 us
    reduce_sum x1, other arithmetic, online_update(): totals = jnp.sum(expo, axis=-1)  44.5 us
  transfers between devices with their start and end apart: 10, of which 9 were waited for; matrix products, arithmetic and copies ran while one was open for 32% of the time, Pallas kernels for 0%

commit v1 on v0

--- a/solution.py
+++ b/solution.py
@@ -4,6 +4,22 @@
 from jax.sharding import PartitionSpec as P
 
 HEAD_DIM = 128
+
+
+def ring_gather(x, axis, dim):
+    ways, here, lap = (lax.axis_size(axis), lax.axis_index(axis), x.shape[dim])
+    dims = [n * ways if d == dim else n for d, n in enumerate(x.shape)]
+    full = lax.dynamic_update_slice_in_dim(jnp.zeros(dims, x.dtype), x, here * lap, axis=dim)
+    going_up = going_down = x
+    for far in range(1, ways // 2 + 1):
+        going_up = lax.ppermute(going_up, axis, [(d, (d + 1) % ways) for d in range(ways)])
+        full = lax.dynamic_update_slice_in_dim(full, going_up, (here - far) % ways * lap, axis=dim)
+        if 2 * far < ways:
+            going_down = lax.ppermute(going_down, axis, [(d, (d - 1) % ways) for d in range(ways)])
+            full = lax.dynamic_update_slice_in_dim(
+                full, going_down, (here + far) % ways * lap, axis=dim
+            )
+    return full
 
 
 def swapped(block, axis, stride):
@@ -51,7 +67,7 @@
     inverse_rms = lax.rsqrt(jnp.mean(flat_rows * flat_rows, axis=1, keepdims=True) + 1e-05)
     normed = (flat_rows * inverse_rms * norm_gain).astype(jnp.bfloat16)
     full_query, full_key, full_value, full_out = (
-        lax.all_gather(query_weight, "seq", axis=0, tiled=True),
+        ring_gather(query_weight, "seq", 0),
         lax.all_gather(key_weight, "seq", axis=0, tiled=True),
         lax.all_gather(value_projection_weight, "seq", axis=0, tiled=True),
         lax.all_gather(out_weight, "seq", axis=1, tiled=True),

time: 666 us -> 805 us (1.21)
  waiting for transfers between devices: 418 us -> 541 us
  local copies, waits for them, and re-layouts: 23.1 us -> 36.8 us
  starting transfers between devices: 3.53 us -> 13 us
    ppermute x0 -> x7, waiting for transfers between devices: none -> 299 us  [the longest x4 293 us: ring_gather(): lax.ppermute(going_up, axis, [(d, (d + 1) % ways) for d in range(ways)])]
    all_gather x1 -> x0, waiting for transfers between devices: 130 us -> none  [body(): lax.all_gather(query_weight, 'seq', axis=0, tiled=True)]
    all_gather x1, waiting for transfers between devices: 47.4 us -> 0.01 us  [body(): lax.all_gather(partner_values, 'seq', axis=1, tiled=True)]
    reduce_scatter x1, waiting for transfers between devices: 53.6 us -> 82.3 us  [body(): lax.psum_scatter(partial_out.astype(jnp.bfloat16), 'tensor', scatter_dime...]
    all_gather x1, waiting for transfers between devices: 27.1 us -> 0.01 us  [body(): lax.all_gather(partner_keys, 'seq', axis=1, tiled=True)]
    ppermute x0 -> x7, starting transfers between devices: none -> 9.69 us  [the longest x3 9.62 us: ring_gather(): lax.ppermute(going_down, axis, [(d, (d - 1) % ways) for d in range(ways)])]
    dynamic_update_slice x0 -> x8, local copies, waits for them, and re-layouts: none -> 8.7 us  [the longest x4 4.26 us: ring_gather(): lax.dynamic_update_slice_in_dim(full, going_up, (here - far) % ways * lap...]
  transfers between devices with their start and end apart: 10 -> 16, of which waited for: 9 -> 11; matrix products, arithmetic and copies ran while one was open for 32% -> 27% of each run, Pallas kernels for 0% -> 0%
where the time goes in v1:
time: 805 us
  waiting for transfers between devices  541 us (67%)
  matrix products  139 us (17%)
  other arithmetic  60.8 us (8%)
  local copies, waits for them, and re-layouts  36.8 us (5%)
  between operations  13.7 us (2%)
  starting transfers between devices  13 us (2%)
    ppermute x4, waiting for transfers between devices, ring_gather(): lax.ppermute(going_up, axis, [(d, (d + 1) % ways) for d in range(ways)])  293 us
    reduce_scatter x1, waiting for transfers between devices, body(): lax.psum_scatter(partial_out.astype(jnp.bfloat16), 'tensor', scatter_dime...  82.3 us
    all_gather x1, waiting for transfers between devices, body(): gathered = lax.all_gather(hidden, 'tensor', axis=3, tiled=True)  59.6 us
    dot_general x1, matrix products, online_update(): jnp.einsum('bkrn,bnkd->bkrd', expo.astype(jnp.bfloat16), value_heads, pre...  53.4 us
    dot_general x1, matrix products, online_update(): jnp.einsum('bkrd,bnkd->bkrn', query_heads, key_heads, preferred_element_t...  49.4 us
    all_gather x1, waiting for transfers between devices, body(): lax.all_gather(key_weight, 'seq', axis=0, tiled=True)  45.7 us
    reduce_sum x1, other arithmetic, online_update(): totals = jnp.sum(expo, axis=-1)  44.6 us
    all_gather x1, waiting for transfers between devices, body(): lax.all_gather(value_projection_weight, 'seq', axis=0, tiled=True)  26.6 us
  transfers between devices with their start and end apart: 16, of which 11 were waited for; matrix products, arithmetic and copies ran while one was open for 27% of the time, Pallas kernels for 0%

profile of v1, /device:TPU:0, one launch (start us, length us, event | category | flops | bytes accessed | tf_op | source)
XLA Modules:
  0.0 804.9 jit_solution(3488407843064601428)
XLA Ops:
  8.8 59.6 %all-gather.7.cloned.1.call-done = bf16[1,1,512,4096]{3,2,1,0:T(8,128)(2,1)} async-done(((bf16[1,1,512,2048]{3,2,1,0:T(8,128)(2,1)}), bf16[1,1,512,4096]{3,2,1,0:T(8,128)(2,1)}) %all-gather.7.cloned.1.call-update) | async-done | bytes 4194320 | tf_op jit(solution)/shard_map/all_gather | solution.py:64
  68.4 3.1 fusion.17
  71.5 45.7 %all-gather.9.cloned.1.call-done = bf16[4096,512]{1,0:T(8,128)(2,1)} async-done(((bf16[512,512]{1,0:T(8,128)(2,1)}), bf16[4096,512]{1,0:T(8,128)(2,1)}) %all-gather.9.cloned.1.call-update) | async-done | bytes 4194320 | tf_op jit(solution)/shard_map/all_gather | solution.py:71
  117.2 5.9 fusion.20
  124.6 12.6 %collective-permute-done.7 = bf16[1,512,512]{2,1,0:T(8,128)(2,1)S(1)} collective-permute-done((bf16[1,512,512]{2,1,0:T(8,128)(2,1)S(1)}, bf16[1,512,512]{2,1,0:T(8,128)(2,1)S(1)}, u32[]{:S(2)}, u32[]{:S(2)}) %collective-permute-start.7) | collective-permute-done | bytes 524320 | tf_op jit(solution)/shard_map/ppermute | solution.py:32
  138.1 26.6 %all-gather.13.cloned.1.call-done = bf16[4096,512]{1,0:T(8,128)(2,1)} async-done(((bf16[512,512]{1,0:T(8,128)(2,1)}), bf16[4096,512]{1,0:T(8,128)(2,1)}) %all-gather.13.cloned.1.call-update) | async-done | bytes 4194320 | tf_op jit(solution)/shard_map/all_gather | solution.py:72
  164.7 5.8 fusion.21
  172.1 12.6 %collective-permute-done.8 = bf16[1,512,512]{2,1,0:T(8,128)(2,1)S(1)} collective-permute-done((bf16[1,512,512]{2,1,0:T(8,128)(2,1)S(1)}, bf16[1,512,512]{2,1,0:T(8,128)(2,1)S(1)}, u32[]{:S(2)}, u32[]{:S(2)}) %collective-permute-start.8) | collective-permute-done | bytes 524320 | tf_op jit(solution)/shard_map/ppermute | solution.py:32
  186.2 3.5 collective-permute-start.1
  189.7 77.2 %collective-permute-done = bf16[512,2048]{1,0:T(8,128)(2,1)S(1)} collective-permute-done((bf16[512,2048]{1,0:T(8,128)(2,1)S(1)}, bf16[512,2048]{1,0:T(8,128)(2,1)S(1)}, u32[]{:S(2)}, u32[]{:S(2)}) %collective-permute-start) | collective-permute-done | bytes 2097184 | tf_op jit(solution)/shard_map/ppermute | solution.py:15
  268.2 2.3 collective-permute-start.3
  270.5 69.5 %collective-permute-done.2 = bf16[512,2048]{1,0:T(8,128)(2,1)S(1)} collective-permute-done((bf16[512,2048]{1,0:T(8,128)(2,1)S(1)}, bf16[512,2048]{1,0:T(8,128)(2,1)S(1)}, u32[]{:S(2)}, u32[]{:S(2)}) %collective-permute-start.2) | collective-permute-done | bytes 2097184 | tf_op jit(solution)/shard_map/ppermute | solution.py:15
  340.0 6.8 collective-permute-done.3
  346.8 3.8 collective-permute-start.5
  350.6 82.7 %collective-permute-done.4 = bf16[512,2048]{1,0:T(8,128)(2,1)} collective-permute-done((bf16[512,2048]{1,0:T(8,128)(2,1)S(1)}, bf16[512,2048]{1,0:T(8,128)(2,1)}, u32[]{:S(2)}, u32[]{:S(2)}) %collective-permute-start.4) | collective-permute-done | bytes 2097184 | tf_op jit(solution)/shard_map/ppermute | solution.py:15
  433.3 2.0 broadcast_in_dim.30
  438.1 2.0 constant_dynamic-update-slice_fusion.3
  443.9 63.2 %collective-permute-done.6 = bf16[512,2048]{1,0:T(8,128)(2,1)} collective-permute-done((bf16[512,2048]{1,0:T(8,128)(2,1)}, bf16[512,2048]{1,0:T(8,128)(2,1)}, u32[]{:S(2)}, u32[]{:S(2)}) %collective-permute-start.6) | collective-permute-done | bytes 2097184 | tf_op jit(solution)/shard_map/ppermute | solution.py:15
  509.0 10.2 %convolution_convert_fusion.1 = bf16[512,2048]{1,0:T(8,128)(2,1)} fusion(bf16[4096,2048]{1,0:T(8,128)(2,1)S(1)} %constant_dynamic-update-slice_fusion, bf16[1,1,512,4096]{3,2,1,0:T(8,128)(2,1)S(1)} %copy-done, f32[4096]{0:T(1024)S(1)} %copy-done.11, f32[512]{0:T(512)S(1)} %add_rsqrt_fusion), kind=kOutput, calls=%fused_computation.24 | convolution fusion | flops 8599371776 | bytes 23087104 | tf_op jit(solution)/shard_map/dot_general | solution.py:75
  519.2 3.4 reshape.72
  522.6 1.9 copy.27
  524.5 171.5 %conditional.1 = (f32[1,4,2048]{2,1,0:T(4,128)}, f32[1,4,2048,128]{3,2,1,0:T(8,128)}) conditional(s32[]{:T(128)} %convert_element_type.33, () %tuple.13, (s32[]{:T(128)}, s32[4,512]{1,0:T(4,128)S(1)}, bf16[1,4,4,512,128]{4,3,2,1,0:T(8,128)(2,1)}, bf16[1,4096,512]{2,1,0:T(8,128)(2,1)}, bf16[1,4096,512]{2,1,0:T(8,128)(2,1)}) %tuple.32), branch_computations={%region_1.2_spmd, %region_2.5_spmd} | conditional | flops 17624459264 | bytes 476291136 | solution.py:110
  524.5 10.2 %iota_compare_fusion = pred[2048,4096]{1,0:T(8,128)(4,1)} fusion(s32[2048]{0:T(1024)S(1)} %bitcast.37), kind=kLoop, calls=%fused_computation.7 | loop fusion | flops 8388608 | bytes 8396800 | tf_op jit(solution)/shard_map/cond/branch_1_fun/le | solution.py:46
  534.7 6.9 reshape.64
  541.6 49.4 %fusion = (f32[4,2048]{1,0:T(4,128)S(1)}, f32[4,2048,4096]{2,1,0:T(8,128)}) fusion(pred[2048,4096]{1,0:T(8,128)(4,1)} %iota_compare_fusion, bf16[4,2048,128]{2,1,0:T(8,128)(2,1)S(1)} %bitcast.35, bf16[4096,4,128]{2,1,0:T(4,128)(2,1)} %reshape.64), kind=kOutput, calls=%fused_computation.2 | convolution fusion | flops 8690589696 | bytes 148930560 | tf_op jit(solution)/shard_map/cond/branch_1_fun/bkrd,bnkd->bkrn/dot_general | solution.py:42
  591.1 6.9 reshape.65
  598.0 53.4 %fusion.9 = f32[1,4,2048,128]{3,2,1,0:T(8,128)} fusion(bf16[4096,4,128]{2,1,0:T(4,128)(2,1)} %reshape.65, f32[4,2048,4096]{2,1,0:T(8,128)} %get-tuple-element.29, f32[4,2048]{1,0:T(4,128)S(1)} %broadcast_maximum_fusion, pred[2048,4096]{1,0:T(8,128)(4,1)} %iota_compare_fusion), kind=kOutput, calls=%fused_computation.11 | convolution fusion | flops 8757706752 | bytes 151027712 | tf_op jit(solution)/shard_map/cond/branch_1_fun/bkrn,bnkd->bkrd/dot_general | solution.py:51
  651.4 44.6 %fusion.2 = f32[4,2048]{1,0:T(4,128)} fusion(f32[4,2048,4096]{2,1,0:T(8,128)} %get-tuple-element.29, f32[4,2048]{1,0:T(4,128)S(1)} %broadcast_maximum_fusion, pred[2048,4096]{1,0:T(8,128)(4,1)} %iota_compare_fusion), kind=kLoop, calls=%fused_computation.4 | loop fusion | flops 167763968 | bytes 142671872 | tf_op jit(solution)/shard_map/cond/branch_1_fun/reduce_sum | solution.py:50
  696.0 2.9 divide_convert_fusion
  698.9 2.3 copy.16
  701.2 14.5 %convolution_convert_fusion = bf16[512,4096]{1,0:T(8,128)(2,1)} fusion(bf16[512,2048]{0,1:T(8,128)(2,1)} %bitcast.36, bf16[2048,4096]{1,0:T(8,128)(2,1)} %all-gather.17.cloned.1.call-done), kind=kOutput, calls=%fused_computation.22 | convolution fusion | flops 8592031744 | bytes 23068672 | tf_op jit(solution)/shard_map/dot_general | solution.py:117
  715.8 82.3 %reduce-scatter.2.cloned.1.call-done = bf16[512,2048]{1,0:T(8,128)(2,1)} async-done(((bf16[512,4096]{1,0:T(8,128)(2,1)}), bf16[512,2048]{1,0:T(8,128)(2,1)}) %reduce-scatter.2.cloned.1.call-update) | async-done | bytes 2097168 | tf_op jit(solution)/shard_map/reduce_scatter | solution.py:118
  (61 shorter events, 17.3 us)
Async XLA Ops:
  6.5 61.8 %all-gather.7.cloned.1.call-start = ((), (), s32[]{:S(2)}) async-start(), calls=%async_computation.1 | async-start | bytes 6291456 | tf_op jit(solution)/shard_map/all_gather | solution.py:64
  7.3 109.9 %all-gather.9.cloned.1.call-start = ((), (), s32[]{:S(2)}) async-start(), calls=%async_computation.2 | async-start | bytes 4718592 | tf_op jit(solution)/shard_map/all_gather | solution.py:71
  8.0 156.7 %all-gather.13.cloned.1.call-start = ((), (), s32[]{:S(2)}) async-start(), calls=%async_computation.4 | async-start | bytes 4718592 | tf_op jit(solution)/shard_map/all_gather | solution.py:72
  8.7 515.7 %all-gather.11.cloned.1.call-start = ((), (), s32[]{:S(2)}) async-start(), calls=%async_computation.3 | async-start | bytes 4718592 | tf_op jit(solution)/shard_map/all_gather | solution.py:100
  71.5 93.2 %copy-start.11 = (f32[4096]{0:T(1024)S(1)}, f32[4096]{0:T(1024)}, u32[]{:S(2)}) copy-start(f32[4096]{0:T(1024)} %param.9) | copy-start | bytes 49156
  123.0 14.1 %collective-permute-start.7 = (bf16[1,512,512]{2,1,0:T(8,128)(2,1)S(1)}, bf16[1,512,512]{2,1,0:T(8,128)(2,1)S(1)}, u32[]{:S(2)}, u32[]{:S(2)}) collective-permute-start(bf16[1,512,512]{2,1,0:T(8,128)(2,1)S(1)} %fusion.20), channel_id=1, source_target_pairs={{0,16},{16,0},{1,17},{17,1},{2,18},{18,2},{3,19},{19,3},{4,20},{20... | collective-permute-start | bytes 1572872 | tf_op jit(solution)/shard_map/ppermute | solution.py:32
  137.2 0.8 copy-start.9
  138.0 48.1 %copy-start.1 = (bf16[512,2048]{1,0:T(8,128)(2,1)S(1)}, bf16[512,2048]{1,0:T(8,128)(2,1)}, u32[]{:S(2)}) copy-start(bf16[512,2048]{1,0:T(8,128)(2,1)} %param.10) | copy-start | bytes 6291460
  138.0 386.4 %all-gather.15.cloned.1.call-start = ((), (), s32[]{:S(2)}) async-start(), calls=%async_computation.5 | async-start | bytes 4718592 | tf_op jit(solution)/shard_map/all_gather | solution.py:101
  170.5 14.1 %collective-permute-start.8 = (bf16[1,512,512]{2,1,0:T(8,128)(2,1)S(1)}, bf16[1,512,512]{2,1,0:T(8,128)(2,1)S(1)}, u32[]{:S(2)}, u32[]{:S(2)}) collective-permute-start(bf16[1,512,512]{2,1,0:T(8,128)(2,1)S(1)} %fusion.21), channel_id=1, source_target_pairs={{0,16},{16,0},{1,17},{17,1},{2,18},{18,2},{3,19},{19,3},{4,20},{20... | collective-permute-start | bytes 1572872 | tf_op jit(solution)/shard_map/ppermute | solution.py:32
  184.7 0.8 copy-start.10
  185.5 515.8 %all-gather.17.cloned.1.call-start = ((), (), s32[]{:S(2)}) async-start(), calls=%async_computation.6 | async-start | bytes 18874368 | tf_op jit(solution)/shard_map/all_gather | solution.py:73
  186.1 612.0 %reduce-scatter.2.cloned.1.call-start = ((), (), s32[]{:S(2)}) async-start(), calls=%async_computation.7 | async-start | bytes 6291456 | tf_op jit(solution)/shard_map/reduce_scatter | solution.py:118
  186.1 80.7 %collective-permute-start = (bf16[512,2048]{1,0:T(8,128)(2,1)S(1)}, bf16[512,2048]{1,0:T(8,128)(2,1)S(1)}, u32[]{:S(2)}, u32[]{:S(2)}) collective-permute-start(bf16[512,2048]{1,0:T(8,128)(2,1)S(1)} %copy-done.1), channel_id=1, source_target_pairs={{0,2},{2,4},{4,6},{6,8},{8,10},{10,12},{12,14},{14,0},{1,3},{3,5},... | collective-permute-start | bytes 6291464 | tf_op jit(solution)/shard_map/ppermute | solution.py:15
  186.2 80.7 %collective-permute-start.1 = (bf16[512,2048]{1,0:T(8,128)(2,1)S(1)}, bf16[512,2048]{1,0:T(8,128)(2,1)S(1)}, u32[]{:S(2)}, u32[]{:S(2)}) collective-permute-start(bf16[512,2048]{1,0:T(8,128)(2,1)S(1)} %copy-done.1), channel_id=1, source_target_pairs={{0,14},{2,0},{4,2},{6,4},{8,6},{10,8},{12,10},{14,12},{1,15},{3,1}... | collective-permute-start | bytes 6291464 | tf_op jit(solution)/shard_map/ppermute | solution.py:18
  266.9 1.3 copy-start.2
  266.9 73.1 %collective-permute-start.2 = (bf16[512,2048]{1,0:T(8,128)(2,1)S(1)}, bf16[512,2048]{1,0:T(8,128)(2,1)S(1)}, u32[]{:S(2)}, u32[]{:S(2)}) collective-permute-start(bf16[512,2048]{1,0:T(8,128)(2,1)S(1)} %collective-permute-done), channel_id=1, source_target_pairs={{0,2},{2,4},{4,6},{6,8},{8,10},{10,12},{12,14},{14,0},{1,3},{3,5},... | collective-permute-start | bytes 6291464 | tf_op jit(solution)/shard_map/ppermute | solution.py:15
  268.2 71.8 %copy-start.4 = (bf16[512,2048]{1,0:T(8,128)(2,1)}, bf16[512,2048]{1,0:T(8,128)(2,1)S(1)}, u32[]{:S(2)}) copy-start(bf16[512,2048]{1,0:T(8,128)(2,1)S(1)} %collective-permute-done.1) | copy-start | bytes 6291460
  268.2 78.6 %collective-permute-start.3 = (bf16[512,2048]{1,0:T(8,128)(2,1)S(1)}, bf16[512,2048]{1,0:T(8,128)(2,1)}, u32[]{:S(2)}, u32[]{:S(2)}) collective-permute-start(bf16[512,2048]{1,0:T(8,128)(2,1)S(1)} %collective-permute-done.1), channel_id=1, source_target_pairs={{0,14},{2,0},{4,2},{6,4},{8,6},{10,8},{12,10},{14,12},{1,15},{3,1}... | collective-permute-start | bytes 6291464 | tf_op jit(solution)/shard_map/ppermute | solution.py:18
  340.0 6.8 copy-start.6
  340.0 93.3 %collective-permute-start.4 = (bf16[512,2048]{1,0:T(8,128)(2,1)S(1)}, bf16[512,2048]{1,0:T(8,128)(2,1)}, u32[]{:S(2)}, u32[]{:S(2)}) collective-permute-start(bf16[512,2048]{1,0:T(8,128)(2,1)S(1)} %collective-permute-done.2), channel_id=1, source_target_pairs={{0,2},{2,4},{4,6},{6,8},{8,10},{10,12},{12,14},{14,0},{1,3},{3,5},... | collective-permute-start | bytes 6291464 | tf_op jit(solution)/shard_map/ppermute | solution.py:15
  346.8 95.2 %collective-permute-start.5 = (bf16[512,2048]{1,0:T(8,128)(2,1)}, bf16[512,2048]{1,0:T(8,128)(2,1)}, u32[]{:S(2)}, u32[]{:S(2)}) collective-permute-start(bf16[512,2048]{1,0:T(8,128)(2,1)} %collective-permute-done.3), channel_id=1, source_target_pairs={{0,14},{2,0},{4,2},{6,4},{8,6},{10,8},{12,10},{14,12},{1,15},{3,1}... | collective-permute-start | bytes 6291464 | tf_op jit(solution)/shard_map/ppermute | solution.py:18
  433.3 73.8 %collective-permute-start.6 = (bf16[512,2048]{1,0:T(8,128)(2,1)}, bf16[512,2048]{1,0:T(8,128)(2,1)}, u32[]{:S(2)}, u32[]{:S(2)}) collective-permute-start(bf16[512,2048]{1,0:T(8,128)(2,1)} %collective-permute-done.4), channel_id=1, source_target_pairs={{0,2},{2,4},{4,6},{6,8},{8,10},{10,12},{12,14},{14,0},{1,3},{3,5},... | collective-permute-start | bytes 6291464 | tf_op jit(solution)/shard_map/ppermute | solution.py:15
  433.3 2.4 copy-start.3
  435.4 1.6 copy-start.5
  435.4 2.4 copy-start.7
  438.1 70.9 %copy-start = (bf16[1,1,512,4096]{3,2,1,0:T(8,128)(2,1)S(1)}, bf16[1,1,512,4096]{3,2,1,0:T(8,128)(2,1)}, u32[]{:S(2)}) copy-start(bf16[1,1,512,4096]{3,2,1,0:T(8,128)(2,1)} %all-gather.7.cloned.1.call-done) | copy-start | bytes 12582916
  524.5 17.1 %copy-start.8 = (bf16[1,4,4,512,128]{4,3,2,1,0:T(8,128)(2,1)S(1)}, bf16[1,4,4,512,128]{4,3,2,1,0:T(8,128)(2,1)}, u32[]{:S(2)}) copy-start(bf16[1,4,4,512,128]{4,3,2,1,0:T(8,128)(2,1)} %get-tuple-element.21) | copy-start | bytes 6291460 | tf_op jit(solution)/shard_map/cond
Sparse Core Ops, SparseCore 0:
  8.9 59.4 all-gather.6
  70.0 47.1 all-gather.8
  118.8 45.8 all-gather.12
  166.1 60.0 all-gather.10
  227.6 77.5 all-gather.14
  306.6 231.2 all-gather.16
  715.9 82.0 reduce-scatter.1
